TPU v7x, 1024 devices: a whole 4x4x32 slice. The times are simulated.
1024 devices in a mesh: dp: 16 (over x, y), expert: 64 (over z, core).
Axes of the slice: x: 4, y: 4, z: 32, core: 2. Of those that a mesh axis runs over, the one named last changes fastest.
Arguments:
- hidden: bfloat16 [2048, 16384], P('dp', 'expert'), may hold values from -6 to 6
- expert_ids: int32 [2048, 8], P(('dp', 'expert')), may hold values from 0 to 15, all different within a row; in each aligned block of 2 rows (0 to 1, 2 to 3, ...) at most 2 rows name the same one
- route_weight: float32 [2048, 8], P(('dp', 'expert')), may hold values from 0.1 to 1
- cotangent: bfloat16 [2048, 7168], P(('dp', 'expert')), may hold values from -6 to 6
- w_down: bfloat16 [16384, 7168], P('expert'), may hold values from -0.1875 to 0.1875
Outputs:
- mixed: bfloat16 [2048, 7168], P(('dp', 'expert'))
- grad_hidden: bfloat16 [2048, 16384], P('dp', 'expert')
- grad_down: bfloat16 [16384, 7168], P('expert', 'dp')
Inputs may be any that keep to these rules, and one draw needn't show every extreme that they name: `expert_ids`: each row names 8 different experts. In each aligned block of 2 rows (the tokens of one device) no expert is named more than 2 times, a bound that some block reaches.
All inputs are finite; a program needn't handle non-finite values.
Results may differ from a plain program's by a relative error of at most 0.018.
Values may be sent and summed in bfloat16 or wider, within the bound.
A program may use at most 32 MiB of HBM per device.

v0:
```python
import jax
import jax.numpy as jnp
from jax import lax
from jax.sharding import PartitionSpec as P


def body(hidden, expert_ids, route_weight, cotangent, w_down):
    tok_dev, feature_width = cotangent.shape
    top_count = expert_ids.shape[1]
    devices = lax.axis_size("expert")
    experts = devices // 4
    capacity = min(tok_dev, max(2, (3 * tok_dev * top_count + 2 * experts - 1) // (2 * experts)))
    routed = tok_dev * top_count
    slot_total = experts * capacity
    row_count = devices * capacity
    chosen = expert_ids.reshape(routed)
    onehot = (chosen[:, None] == jnp.arange(experts, dtype=jnp.int32)[None, :]).astype(jnp.int32)
    position = jnp.sum(jnp.cumsum(onehot, axis=0) * onehot, axis=1) - 1
    slot_index = chosen * capacity + position
    placer = (slot_index[:, None] == jnp.arange(slot_total, dtype=jnp.int32)[None, :]).astype(
        jnp.bfloat16
    )
    first_dims = (((0,), (0,)), ((), ()))
    last_dims = (((1,), (1,)), ((), ()))
    quarter_out = jnp.dot(hidden, w_down, preferred_element_type=jnp.float32).astype(jnp.bfloat16)
    out_back = lax.all_to_all(
        quarter_out.reshape(devices, capacity, feature_width),
        "expert",
        split_axis=0,
        concat_axis=0,
        tiled=True,
    )
    scaled = (route_weight[:, :, None] * cotangent.astype(jnp.float32)[:, None, :]).astype(
        jnp.bfloat16
    )
    grad_buffer = lax.dot_general(
        placer,
        scaled.reshape(routed, feature_width),
        first_dims,
        preferred_element_type=jnp.float32,
    ).astype(jnp.bfloat16)
    spread = jnp.broadcast_to(
        grad_buffer.reshape(experts, 1, capacity, feature_width),
        (experts, 4, capacity, feature_width),
    ).reshape(devices, capacity, feature_width)
    grad_recv = lax.all_to_all(spread, "expert", split_axis=0, concat_axis=0, tiled=True)
    grad_rows = grad_recv.reshape(row_count, feature_width)
    grad_hidden = lax.dot_general(
        grad_rows, w_down, last_dims, preferred_element_type=jnp.float32
    ).astype(jnp.bfloat16)
    weight_term = lax.dot_general(hidden, grad_rows, first_dims, preferred_element_type=jnp.float32)
    grad_down = lax.psum_scatter(
        weight_term.astype(jnp.bfloat16), "dp", scatter_dimension=1, tiled=True
    )
    received = out_back.reshape(experts, 4, capacity, feature_width)
    gathered = jnp.zeros((routed, feature_width), jnp.float32)
    for quarter in range(4):
        gathered = gathered + jnp.dot(
            placer,
            received[:, quarter].reshape(slot_total, feature_width),
            preferred_element_type=jnp.float32,
        )
    mixed = jnp.sum(
        route_weight[:, :, None] * gathered.reshape(tok_dev, top_count, feature_width), axis=1
    ).astype(jnp.bfloat16)
    return (mixed, grad_hidden, grad_down)


def solution(mesh):
    return jax.shard_map(
        body,
        mesh=mesh,
        in_specs=(
            P("dp", "expert"),
            P(("dp", "expert"), None),
            P(("dp", "expert"), None),
            P(("dp", "expert"), None),
            P("expert", None),
        ),
        out_specs=(P(("dp", "expert"), None), P("dp", "expert"), P("expert", "dp")),
        check_vma=False,
    )
```

profile of v0, /device:TPU:1, one launch (start us, length us, event | category | flops | bytes accessed | tf_op | source)
XLA Modules:
  0.0 420.6 jit_solution(9512415494448880132)
XLA Ops:
  7.2 0.8 reshape.41
  8.0 0.8 mul.40
  8.8 0.2 select_reduce_fusion
  9.0 0.8 convert_element_type.32
  9.8 0.4 convolution_convert_fusion.2
  10.2 0.2 broadcast_in_dim.4
  10.4 2.2 broadcast_in_dim.5
  12.6 30.4 %all-to-all-start.1 = ((bf16[64,2,7168]{2,1,0:T(2,128)(2,1)}), bf16[64,2,7168]{2,1,0:T(2,128)(2,1)S(1)}, u32[]{:S(2)}, u32[]{:S(2)}) async-start(bf16[64,2,7168]{2,1,0:T(2,128)(2,1)} %bitcast.25), calls=%async_computation.1 | async-start | bytes 3670016 | tf_op jit(solution)/shard_map/all_to_all | solution.py:46
  43.0 3.9 convolution_convert_fusion.1
  46.9 4.8 %reshape.42 = bf16[64,2,7168]{2,1,0:T(2,128)(2,1)} reshape(bf16[128,7168]{1,0:T(8,128)(2,1)} %convolution_convert_fusion.1) | data formatting | bytes 3670016 | tf_op jit(solution)/shard_map/reshape | solution.py:27
  51.7 166.8 %all-to-all-done.1 = bf16[64,2,7168]{2,1,0:T(2,128)(2,1)S(1)} async-done(((bf16[64,2,7168]{2,1,0:T(2,128)(2,1)}), bf16[64,2,7168]{2,1,0:T(2,128)(2,1)S(1)}, u32[]{:S(2)}, u32[]{:S(2)}) %all-to-all-start.1) | async-done | bytes 1835040 | tf_op jit(solution)/shard_map/all_to_all | solution.py:46
  218.5 8.0 %all-to-all-start = ((bf16[64,2,7168]{2,1,0:T(2,128)(2,1)}), bf16[64,2,7168]{2,1,0:T(2,128)(2,1)}, u32[]{:S(2)}, u32[]{:S(2)}) async-start(bf16[64,2,7168]{2,1,0:T(2,128)(2,1)} %reshape.42), calls=%async_computation | async-start | bytes 3670016 | tf_op jit(solution)/shard_map/all_to_all | solution.py:26
  226.5 4.1 reshape.46
  230.6 2.9 fusion
  233.6 167.7 %all-to-all-done = bf16[64,2,7168]{2,1,0:T(2,128)(2,1)} async-done(((bf16[64,2,7168]{2,1,0:T(2,128)(2,1)}), bf16[64,2,7168]{2,1,0:T(2,128)(2,1)}, u32[]{:S(2)}, u32[]{:S(2)}) %all-to-all-start) | async-done | bytes 1835040 | tf_op jit(solution)/shard_map/all_to_all | solution.py:26
  401.3 3.5 fusion.15
  404.7 2.0 reshape_squeeze.15
  406.7 0.9 reshape_squeeze.14
  407.6 1.0 reshape_squeeze.13
  408.8 0.3 fusion.8
  409.1 1.4 convolution_add_fusion.2
  410.5 0.3 convolution_add_fusion.1
  410.8 1.0 fusion.3
  411.8 2.0 convolution_convert_fusion.3
  (19 shorter events, 0.4 us)
Async XLA Ops:
  7.2 35.8 %copy-start = (bf16[128,256]{1,0:T(8,128)(2,1)S(1)}, bf16[128,256]{1,0:T(8,128)(2,1)}, u32[]{:S(2)}) copy-start(bf16[128,256]{1,0:T(8,128)(2,1)} %param.5) | copy-start | bytes 196612
  12.6 205.9 %all-to-all-start.1 = ((bf16[64,2,7168]{2,1,0:T(2,128)(2,1)}), bf16[64,2,7168]{2,1,0:T(2,128)(2,1)S(1)}, u32[]{:S(2)}, u32[]{:S(2)}) async-start(bf16[64,2,7168]{2,1,0:T(2,128)(2,1)} %bitcast.25), calls=%async_computation.1 | async-start | bytes 3670016 | tf_op jit(solution)/shard_map/all_to_all | solution.py:46
  218.5 8.0 %copy-start.2 = (bf16[64,2,7168]{2,1,0:T(2,128)(2,1)}, bf16[64,2,7168]{2,1,0:T(2,128)(2,1)S(1)}, u32[]{:S(2)}) copy-start(bf16[64,2,7168]{2,1,0:T(2,128)(2,1)S(1)} %all-to-all-done.1) | copy-start | bytes 5505028
  218.5 182.8 %all-to-all-start = ((bf16[64,2,7168]{2,1,0:T(2,128)(2,1)}), bf16[64,2,7168]{2,1,0:T(2,128)(2,1)}, u32[]{:S(2)}, u32[]{:S(2)}) async-start(bf16[64,2,7168]{2,1,0:T(2,128)(2,1)} %reshape.42), calls=%async_computation | async-start | bytes 3670016 | tf_op jit(solution)/shard_map/all_to_all | solution.py:26
  226.5 187.3 %reduce-scatter.2.cloned.1.call-start = ((), (), s32[]{:S(2)}) async-start(), calls=%async_computation.3 | async-start | bytes 3899392 | tf_op jit(solution)/shard_map/reduce_scatter | solution.py:52
  408.6 1.9 copy-start.4
  408.8 2.0 copy-start.3
  408.8 2.0 copy-start.5
  409.1 2.8 copy-start.1
Sparse Core Ops, SparseCore 0:
  233.7 111.1 reduce-scatter.1
where the time goes:
time: 424 us; the launch traced here: 421 us
  waiting for transfers between devices  335 us (79%)
  starting transfers between devices  38.4 us (9%)
  local copies, waits for them, and re-layouts  20.3 us (5%)
  between operations  14.2 us (3%)
  matrix products  12.2 us (3%)
    all_to_all x1, waiting for transfers between devices, body(): lax.all_to_all(quarter_out.reshape(devices, capacity, feature_width), 'ex...  168 us
    all_to_all x1, waiting for transfers between devices, body(): lax.all_to_all(spread, 'expert', split_axis=0, concat_axis=0, tiled=True)  167 us
    all_to_all x1, starting transfers between devices, body(): lax.all_to_all(spread, 'expert', split_axis=0, concat_axis=0, tiled=True)  30.4 us
  transfers between devices with their start and end apart: 3, of which 2 were waited for; matrix products, arithmetic and copies ran while one was open for 7% of the time, Pallas kernels for 0%

commit v1 on v0

v1 whole, which is shorter than its diff:
```python
import jax
import jax.numpy as jnp
from jax import lax
from jax.sharding import PartitionSpec as P


def body(hidden, expert_ids, route_weight, cotangent, w_down):
    tok_dev, width = cotangent.shape
    devices = lax.axis_size("expert")
    experts = devices // 4
    mine = lax.axis_index("expert") // 4
    onehot = (expert_ids[:, :, None] == jnp.arange(experts, dtype=jnp.int32)).astype(jnp.float32)
    named = jnp.sum(onehot, axis=1)
    weight = jnp.sum(onehot * route_weight[:, :, None], axis=1)
    table = lax.all_gather(jnp.concatenate([named, weight], axis=1), "expert", axis=0, tiled=True)
    rows = lax.all_gather(cotangent, "expert", axis=0, tiled=True)
    n_all = lax.dynamic_index_in_dim(table, mine, axis=1, keepdims=False).reshape(devices, 2)
    w_all = lax.dynamic_index_in_dim(table, mine + experts, axis=1, keepdims=False).reshape(devices, 2)
    n0, n1, w0, w1 = n_all[:, 0:1], n_all[:, 1:2], w_all[:, 0:1], w_all[:, 1:2]
    pairs = hidden.astype(jnp.float32).reshape(devices, 2, -1)
    h0, h1 = pairs[:, 0], pairs[:, 1]
    hw = jnp.stack([w0 * h0, w1 * jnp.where(n0 > 0, h1, h0)], axis=1)
    hw = hw.reshape(2 * devices, -1).astype(jnp.bfloat16)
    out = jnp.dot(hw, w_down, preferred_element_type=jnp.float32).astype(jnp.bfloat16)
    mixed = lax.psum_scatter(out, "expert", scatter_dimension=0, tiled=True)
    term = lax.dot_general(hw, rows, (((0,), (0,)), ((), ())), preferred_element_type=jnp.float32)
    grad_down = lax.psum_scatter(term.astype(jnp.bfloat16), "dp", scatter_dimension=1, tiled=True)
    back = lax.dot_general(rows, w_down, (((1,), (1,)), ((), ())), preferred_element_type=jnp.float32)
    back = back.reshape(devices, 2, -1)
    g0, g1 = w0 * back[:, 0], w1 * back[:, 1]
    first = jnp.where(n0 > 0, g0, g1)
    second = jnp.where(n0 * n1 > 0, g1, 0.0)
    grad_hidden = jnp.stack([first, second], axis=1).reshape(2 * devices, -1).astype(jnp.bfloat16)
    return (mixed, grad_hidden, grad_down)


def solution(mesh):
    return jax.shard_map(
        body,
        mesh=mesh,
        in_specs=(
            P("dp", "expert"),
            P(("dp", "expert"), None),
            P(("dp", "expert"), None),
            P(("dp", "expert"), None),
            P("expert", None),
        ),
        out_specs=(P(("dp", "expert"), None), P("dp", "expert"), P("expert", "dp")),
        check_vma=False,
    )
```

time: 424 us -> 676 us (1.59)
  waiting for transfers between devices: 335 us -> 568 us
  blocking collectives: 0 us -> 70.2 us
  starting transfers between devices: 38.4 us -> 0.12 us
  local copies, waits for them, and re-layouts: 20.3 us -> 9.17 us
    unnamed x1 -> x4, waiting for transfers between devices: 0.02 us -> 389 us
    all_to_all x2 -> x0, waiting for transfers between devices: 334 us -> none  [the longest x1 168 us: body(): lax.all_to_all(quarter_out.reshape(devices, capacity, feature_width), 'ex...]
    reduce_scatter x1, waiting for transfers between devices: 0.01 us -> 108 us  [body(): lax.psum_scatter(term.astype(jnp.bfloat16), 'dp', scatter_dimension=1, ti...]
    all_gather x0 -> x1, waiting for transfers between devices: none -> 70.9 us  [body(): rows = lax.all_gather(cotangent, 'expert', axis=0, tiled=True)]
    all_gather x0 -> x1, blocking collectives: none -> 70.2 us  [body(): lax.all_gather(jnp.concatenate([named, weight], axis=1), 'expert', axis=0...]
    all_to_all x2 -> x0, starting transfers between devices: 38.4 us -> none  [the longest x1 30.4 us: body(): lax.all_to_all(spread, 'expert', split_axis=0, concat_axis=0, tiled=True)]
    reshape x3 -> x4, local copies, waits for them, and re-layouts: 9.61 us -> 1.25 us  [the longest x1 0.91 us: body(): pairs = hidden.astype(jnp.float32).reshape(devices, 2, -1)]
    unnamed x12 -> x4, local copies, waits for them, and re-layouts: 0.03 us -> 7.05 us
  transfers between devices with their start and end apart: 3 -> 3, of which waited for: 2 -> 3; matrix products, arithmetic and copies ran while one was open for 7% -> 3% of each run, Pallas kernels for 0% -> 0%
where the time goes in v1:
time: 676 us; the launch traced here: 675 us
  waiting for transfers between devices  568 us (84%)
  blocking collectives  70.2 us (10%)
  between operations  14.5 us (2%)
  matrix products  10.3 us (2%)
  local copies, waits for them, and re-layouts  9.17 us (1%)
    unnamed x4, waiting for transfers between devices  389 us
    reduce_scatter x1, waiting for transfers between devices, body(): lax.psum_scatter(term.astype(jnp.bfloat16), 'dp', scatter_dimension=1, ti...  108 us
    all_gather x1, waiting for transfers between devices, body(): rows = lax.all_gather(cotangent, 'expert', axis=0, tiled=True)  70.9 us
    all_gather x1, blocking collectives, body(): lax.all_gather(jnp.concatenate([named, weight], axis=1), 'expert', axis=0...  70.2 us
  transfers between devices with their start and end apart: 3, of which 3 were waited for; matrix products, arithmetic and copies ran while one was open for 3% of the time, Pallas kernels for 0%

profile of v1, /device:TPU:1, one launch (start us, length us, event | category | flops | bytes accessed | tf_op | source)
XLA Modules:
  0.0 674.8 jit_solution(2975006601991490202)
XLA Ops:
  7.2 0.7 all-gather.4.cloned.1.call-update
  8.0 0.8 convert_reduce_fusion
  8.8 70.2 %all-gather = f32[64,2,32]{2,1,0:T(2,128)S(1)} all-gather(f32[1,2,32]{2,1,0:T(2,128)S(1)} %maximum_bitcast_fusion), channel_id=1, replica_groups=mesh['dp'=16,'expert'=64] {'expert'}, dimensions={0}, use_global_device_ids=true | all-gather | bytes 16640 | tf_op jit(solution)/shard_map/all_gather | solution.py:15
  79.0 0.2 dynamic-slice_reduce_fusion.1
  79.2 0.1 reshape.77
  79.3 0.1 reshape.80
  79.5 0.9 reshape.83
  80.4 0.2 slice_reduce_fusion.1
  80.5 0.2 fusion.3
  80.7 0.3 multiply_convert_fusion.1
  81.0 0.2 pad_maximum_fusion
  81.2 4.0 convolution_convert_fusion.1
  85.3 70.9 %all-gather.4.cloned.1.call-done = bf16[64,2,7168]{2,1,0:T(2,128)(2,1)} async-done(((bf16[1,2,7168]{2,1,0:T(2,128)(2,1)}), bf16[64,2,7168]{2,1,0:T(2,128)(2,1)}) %all-gather.4.cloned.1.call-update) | async-done | bytes 1835024 | tf_op jit(solution)/shard_map/all_gather | solution.py:16
  156.2 4.1 reshape.87
  160.2 3.0 convolution_convert_fusion
  163.2 1.3 dynamic-slice
  165.2 388.4 %all-reduce.3.cloned.1.call-done = bf16[128,7168]{1,0:T(8,128)(2,1)} async-done(((bf16[128,7168]{1,0:T(8,128)(2,1)}), bf16[128,7168]{1,0:T(8,128)(2,1)}) %all-reduce.3.cloned.1.call-update) | async-done | bytes 1835024
  553.6 1.5 constant_dynamic-slice_fusion
  555.1 3.4 fusion.4
  558.6 0.3 fusion.1
  558.8 0.1 fusion
  559.0 0.2 pad_maximum_fusion.1
  559.2 0.7 convert_element_type.21
  559.8 108.4 %reduce-scatter.2.cloned.1.call-done = bf16[256,448]{0,1:T(8,128)(2,1)} async-done(((bf16[256,7168]{0,1:T(8,128)(2,1)}), bf16[256,448]{0,1:T(8,128)(2,1)}) %reduce-scatter.2.cloned.1.call-update) | async-done | bytes 229392 | tf_op jit(solution)/shard_map/reduce_scatter | solution.py:27
  (8 shorter events, 0.3 us)
Async XLA Ops:
  7.2 149.0 %all-gather.4.cloned.1.call-start = ((), (), s32[]{:S(2)}) async-start(), calls=%async_computation.2 | async-start | bytes 1863680 | tf_op jit(solution)/shard_map/all_gather | solution.py:16
  7.9 545.7 %all-reduce.3.cloned.1.call-start = ((), (), s32[]{:S(2)}) async-start(), calls=%async_computation.3 | async-start | bytes 3670016
  85.2 583.0 %reduce-scatter.2.cloned.1.call-start = ((), (), s32[]{:S(2)}) async-start(), calls=%async_computation.1 | async-start | bytes 3899392 | tf_op jit(solution)/shard_map/reduce_scatter | solution.py:27
Sparse Core Ops, SparseCore 0:
  10.7 145.4 all-gather.3
  158.5 395.0 all-reduce.2
  560.4 107.7 reduce-scatter.1

commit v2 on v1

v2 whole, which is shorter than its diff:
```python
import functools

import jax
import jax.numpy as jnp
from jax import lax
from jax.experimental import pallas as pl
from jax.experimental.pallas import tpu as pltpu
from jax.sharding import PartitionSpec as P

MESH = pl.DeviceIdType.MESH
F32, BF16 = jnp.float32, jnp.bfloat16
NT = (((1,), (1,)), ((), ()))
TN = (((0,), (0,)), ((), ()))
LAG = 4


def onehot(rows, columns, dtype):
    return (rows == columns).astype(F32).astype(dtype)


def kernel(nd, ne, radix, tok_ref, hid_ref, tab_ref, w_ref, mixed_ref, gh_ref, gd_ref,
           w2, sib_tok, merge, sib_hid, table, flat, ring, y_buf, rs_in, rs_out, fin, mix_in,
           hw_t, blocks, g_acc, gh_send, gh_in, acc, acc_in,
           local_sem, sib_s, sib_r, r1_s, r1_r, r2_s, r2_r, ag_s, ag_r, rs_s, rs_r,
           hw_s, hw_r, bl_s, bl_r):
    nz, half = ne // 2, ne // 4
    toks = 4 * half
    units = hid_ref.shape[1]
    tiles = w2.shape[2] // 128
    d, p = lax.axis_index("dp"), lax.axis_index("expert")
    z, c = p // 2, lax.rem(p, 2)
    way = 1 - 2 * c
    expert = p // 4
    base = 1 - c
    sibling = (d, p + 1 - 2 * c)
    ahead = (d, lax.rem(z + way + nz, nz) * 2 + c)
    behind = (d, lax.rem(z - way + nz, nz) * 2 + c)
    groups = ne // radix
    group, member = p // radix, lax.rem(p, radix)

    def copy(src, dst, send, recv, to):
        return pltpu.make_async_remote_copy(src_ref=src, dst_ref=dst, send_sem=send, recv_sem=recv,
                                            device_id=to, device_id_type=MESH)

    w_own = pltpu.make_async_copy(w_ref, w2.at[0], local_sem.at[0])
    w_own.start()

    barrier = pltpu.get_barrier_semaphore()
    for to in (sibling, ahead, behind):
        pl.semaphore_signal(barrier, inc=1, device_id=to, device_id_type=MESH)

    def greet_member(i, _):
        to = (d, group * radix + lax.rem(member + i, radix))
        pl.semaphore_signal(barrier, inc=1, device_id=to, device_id_type=MESH)
        return 0

    def greet_group(i, _):
        to = (d, lax.rem(p + i * radix, ne))
        pl.semaphore_signal(barrier, inc=1, device_id=to, device_id_type=MESH)
        return 0

    def greet_dp(i, _):
        pl.semaphore_signal(barrier, inc=1, device_id=(lax.rem(d + i, nd), p), device_id_type=MESH)
        return 0

    lax.fori_loop(1, radix, greet_member, 0)
    lax.fori_loop(1, groups, greet_group, 0)
    lax.fori_loop(1, nd, greet_dp, 0)
    table[p] = tab_ref[...]
    merge[:, pl.ds(pl.multiple_of(8 * c, 8), 8), :] = tok_ref[...].astype(F32).reshape(nd, 8, 128)
    pl.semaphore_wait(barrier, 3 + (radix - 1) + (groups - 1) + (nd - 1))

    tok_copy = copy(tok_ref, sib_tok, sib_s.at[0], sib_r.at[0], sibling)
    hid_copy = copy(hid_ref, sib_hid, sib_s.at[1], sib_r.at[1], sibling)
    w_copy = copy(w_ref, w2.at[1], sib_s.at[2], sib_r.at[2], sibling)
    tok_copy.start()

    def one(i, back):
        to = lax.rem(member + i, radix)
        slot = group * radix + lax.rem(member + radix - i, radix) if back else p
        return copy(table.at[p], table.at[slot], r1_s.at[i], r1_r.at[i], (d, group * radix + to))

    def two(i, back):
        to = lax.rem(p + i * radix, ne)
        slot = lax.rem(group + groups - i, groups) if back else group
        return copy(table.at[pl.ds(group * radix, radix)], table.at[pl.ds(slot * radix, radix)],
                    r2_s.at[i], r2_r.at[i], (d, to))

    def each(low, high, step):
        def run(i, _):
            step(i)
            return 0
        lax.fori_loop(low, high, run, 0)

    each(1, radix, lambda i: one(i, False).start())
    hid_copy.start()
    w_copy.start()

    def ag(t):
        return copy(ring.at[t], ring.at[t + 1], ag_s.at[t], ag_r.at[t], ahead)

    def rs(t):
        return copy(rs_out.at[t], rs_in.at[t + 1], rs_s.at[t], rs_r.at[t], behind)

    def ag_step(t):
        ag(t - 1).wait_recv()
        if isinstance(t, int) and t == half - 1:
            @pl.when(c == 0)
            def _():
                ag(t).start()
        else:
            ag(t).start()

    tok_copy.wait_recv()
    merge[:, pl.ds(pl.multiple_of(8 * (1 - c), 8), 8), :] = sib_tok[...].astype(F32).reshape(nd, 8, 128)
    ring[0] = merge[...].reshape(16 * nd, 128).astype(BF16)
    ag(0).start()

    each(1, radix, lambda i: one(i, True).wait_recv())
    each(1, groups, lambda i: two(i, False).start())
    done = 1
    if done < half:
        ag_step(done)
        done += 1
    each(1, groups, lambda i: two(i, True).wait_recv())
    hid_copy.wait_recv()

    def flatten(i):
        flat[pl.ds(2 * i, 2), :] = table[i]
    for i in range(ne):
        flatten(i)
    row = lax.broadcasted_iota(jnp.int32, (toks, 4 * nz), 0)
    column = lax.broadcasted_iota(jnp.int32, (toks, 4 * nz), 1)

    def place_of(token):
        chip = z - way * ((token >> 2) + base)
        chip = jnp.where(chip < 0, chip + nz, chip)
        chip = jnp.where(chip >= nz, chip - nz, chip)
        return chip * 4 + (token & 3)

    place = place_of(row)
    picked = jnp.dot(onehot(place, column, F32), flat[...], preferred_element_type=F32,
                     precision=lax.Precision.HIGHEST)
    lane = lax.broadcasted_iota(jnp.int32, (toks, 128), 1)

    def coefficient(k):
        return jnp.sum(jnp.where(lane == expert + 32 * k, picked, 0.0), axis=1, keepdims=True)

    keep, shift, give = coefficient(0), coefficient(1), coefficient(2)
    both = jnp.concatenate([hid_ref[...], sib_hid[...]], axis=1)
    at = jnp.dot(onehot(place, column, BF16), both, preferred_element_type=F32)
    before = jnp.dot(onehot(place - 1, column, BF16), both, preferred_element_type=F32)
    hw = (keep * at + shift * before).astype(BF16)
    spot_row = lax.broadcasted_iota(jnp.int32, (toks, 2 * toks), 0)
    spot_column = lax.broadcasted_iota(jnp.int32, (toks, 2 * toks), 1)
    turned = lax.dot_general(hw[:, :units], onehot(spot_row, spot_column, BF16), TN, preferred_element_type=F32)
    turned = turned + lax.dot_general(hw[:, units:], onehot(spot_row + toks, spot_column, BF16), TN,
                                      preferred_element_type=F32)
    hw_t[d] = turned.astype(BF16)

    def hw_copy(i, back):
        slot = lax.rem(d + nd - i, nd) if back else d
        return copy(hw_t.at[d], hw_t.at[slot], hw_s.at[i], hw_r.at[i], (lax.rem(d + i, nd), p))

    each(1, nd, lambda i: hw_copy(i, False).start())
    if done < half:
        ag_step(done)
        done += 1

    w_own.wait()
    w_copy.wait_recv()

    def forward(m):
        at_column = pl.multiple_of(m * 896, 128)
        columns = w2[:, :, pl.ds(at_column, 896)].reshape(2 * units, 896)
        part = jnp.dot(hw, columns, preferred_element_type=F32)
        for k in range(7):
            y_buf[pl.ds(m * 7 + k, toks, stride=tiles), :] = part[:, 128 * k:128 * k + 128]

    each(0, nd // 4, forward)
    if done < half:
        ag_step(done)
        done += 1
    each(nd // 4, nd // 2, forward)

    def y_at(t):
        return y_buf[pl.ds(pl.multiple_of((half - 1 - t) * 4 * tiles, 8), 4 * tiles), :]

    def rs_step(t):
        rs(t - 1).wait_recv()
        rs_out[t] = (y_at(t) + rs_in[t].astype(F32)).astype(BF16)
        rs(t).start()

    rs_out[0] = y_at(0).astype(BF16)
    rs(0).start()
    last = half - 1
    lag = done - 1
    split = max(1, half - 1 - lag)

    def both_steps(t):
        ag_step(t + lag)
        rs_step(t)

    each(1, split, both_steps)
    if done < half:
        ag_step(last)

    @pl.when(c == 0)
    def _():
        ag(last).wait_recv()

    def block_copy(i, back):
        to = lax.rem(d + i, nd)
        slot = lax.rem(d + nd - i, nd) if back else d
        return copy(ring.at[pl.ds(base, half), pl.ds(pl.multiple_of(16 * to, 16), 16), :], blocks.at[slot],
                    bl_s.at[i], bl_r.at[i], (to, p))

    each(1, nd, lambda i: block_copy(i, False).start())
    own_block = pltpu.make_async_copy(
        ring.at[pl.ds(base, half), pl.ds(pl.multiple_of(16 * d, 16), 16), :], blocks.at[d], local_sem.at[1])
    own_block.start()

    quarter = lax.broadcasted_iota(jnp.int32, (16 * half, 128), 0) & 3

    def spread(values, first):
        return [jnp.where(quarter == k, values, jnp.zeros_like(values)) for k in range(first, 4)]

    g_acc[...] = jnp.zeros_like(g_acc)

    def backward(m):
        at_column = pl.multiple_of(m * 896, 128)
        columns = w2[:, :, pl.ds(at_column, 896)].reshape(2 * units, 896)
        even = ring[pl.ds(base, half), pl.ds(pl.multiple_of(32 * m, 16), 16), :].reshape(16 * half, 128)
        odd = ring[pl.ds(base, half), pl.ds(pl.multiple_of(32 * m + 16, 16), 16), :].reshape(16 * half, 128)
        wide = jnp.concatenate(spread(even, 0) + spread(odd, 1), axis=1)
        g_acc[...] += lax.dot_general(wide, columns, NT, preferred_element_type=F32)

    rest = list(range(split, last))
    per = -(-(nd // 2) // max(1, len(rest) + 1))
    begun = 0
    for t in rest:
        rs_step(t)
        each(begun, min(begun + per, nd // 2), backward)
        begun = min(begun + per, nd // 2)

    rs(last - 1).wait_recv()

    @pl.when(c == 0)
    def _():
        rs_out[last] = (y_at(last) + rs_in[last].astype(F32)).astype(BF16)
        rs(last).start()

    @pl.when(c == 1)
    def _():
        fin[...] = y_at(last) + rs_in[last].astype(F32)

    each(begun, nd // 2, backward)

    @pl.when(c == 0)
    def _():
        rs(last).wait_recv()
        fin[...] = rs_in[last + 1].astype(F32)

    mix_copy = copy(fin.at[pl.ds(pl.multiple_of(2 * tiles * (1 - c), 8), 2 * tiles)], mix_in,
                    sib_s.at[3], sib_r.at[3], sibling)
    mix_copy.start()

    fours = onehot(lax.broadcasted_iota(jnp.int32, (toks, 16 * half), 0),
                   lax.broadcasted_iota(jnp.int32, (toks, 16 * half), 1) >> 2, F32)
    back = jnp.dot(fours, g_acc[...], preferred_element_type=F32, precision=lax.Precision.HIGHEST)
    slots = (keep * back + give * pltpu.roll(back, toks - 1, 0)).astype(BF16)
    home = place_of(lax.broadcasted_iota(jnp.int32, (4 * nz, toks), 1))
    home_row = lax.broadcasted_iota(jnp.int32, (4 * nz, toks), 0)
    placed = jnp.dot(onehot(home, home_row, BF16), slots, preferred_element_type=F32).astype(BF16)
    gh_send[...] = placed[:, units:]
    gh_copy = copy(gh_send, gh_in, sib_s.at[4], sib_r.at[4], sibling)
    gh_copy.start()

    repeat_row = lax.broadcasted_iota(jnp.int32, (2 * toks, 16 * half), 0)
    repeat_column = lax.broadcasted_iota(jnp.int32, (2 * toks, 16 * half), 1) >> 2
    repeat_own = onehot(repeat_row, repeat_column, BF16)
    repeat_sib = onehot(repeat_row, repeat_column + toks, BF16)

    def add_block(slot):
        left = jnp.concatenate([
            jnp.dot(hw_t[slot], repeat_own, preferred_element_type=F32),
            jnp.dot(hw_t[slot], repeat_sib, preferred_element_type=F32)], axis=0).astype(BF16)
        wide = jnp.concatenate(spread(blocks[slot].reshape(16 * half, 128), 0), axis=1)
        return jnp.dot(left, wide, preferred_element_type=F32)

    own_block.wait()
    acc[...] = add_block(d)

    def peer(i):
        hw_copy(i, True).wait_recv()
        block_copy(i, True).wait_recv()
        acc[...] += add_block(lax.rem(d + nd - i, nd))

    each(1, nd, peer)
    acc_copy = copy(acc.at[pl.ds(units, units)], acc_in, sib_s.at[5], sib_r.at[5], sibling)
    acc_copy.start()

    mix_copy.wait_recv()
    own_rows = fin[pl.ds(pl.multiple_of(2 * tiles * c, 8), 2 * tiles), :]
    mixed_ref[...] = (own_rows + mix_in[...]).astype(BF16)
    gh_copy.wait_recv()
    gh_ref[...] = (placed[:, :units].astype(F32) + gh_in[...].astype(F32)).astype(BF16)
    acc_copy.wait_recv()
    total = acc[pl.ds(0, units), :] + acc_in[...]
    gd_ref[...] = jnp.where(lax.rem(d, 2) == 1, total[:, 64:512], total[:, 0:448]).astype(BF16)

    for sent in (tok_copy, hid_copy, w_copy, mix_copy, gh_copy, acc_copy):
        sent.wait_send()
    each(1, radix, lambda i: one(i, False).wait_send())
    each(1, groups, lambda i: two(i, False).wait_send())
    each(0, last, lambda t: ag(t).wait_send())
    each(0, last, lambda t: rs(t).wait_send())

    @pl.when(c == 0)
    def _():
        ag(last).wait_send()
        rs(last).wait_send()

    each(1, nd, lambda i: hw_copy(i, False).wait_send())
    each(1, nd, lambda i: block_copy(i, False).wait_send())


def body(hidden, expert_ids, route_weight, cotangent, w_down):
    width = cotangent.shape[1]
    units = hidden.shape[1]
    nd, ne = lax.axis_size("dp"), lax.axis_size("expert")
    nz, half, tiles = ne // 2, ne // 4, width // 128
    toks = 4 * half
    radix = 8 if ne >= 64 else 4
    chosen = expert_ids[:, :, None] == jnp.arange(32, dtype=jnp.int32)
    named = jnp.any(chosen, axis=1)
    weight = jnp.sum(jnp.where(chosen, route_weight[:, :, None], 0.0), axis=1)
    zero = jnp.zeros_like(weight[0])
    keep = jnp.stack([weight[0], jnp.where(named[0], weight[1], zero)])
    moved = jnp.where(named[0], zero, weight[1])
    table = jnp.concatenate([keep, jnp.stack([zero, moved]), jnp.stack([moved, zero]), jnp.zeros((2, 32), F32)], axis=1)
    pieces = cotangent.reshape(2, nd // 2, 7, 128)
    pieces = jnp.stack([pieces[:, :, 0:4], pieces[:, :, 3:7]], axis=2).reshape(2, nd, 4, 128)
    tokens = pieces.transpose(1, 0, 2, 3).reshape(8 * nd, 128)
    vmem = pl.BlockSpec(memory_space=pltpu.VMEM)
    dma = lambda n: pltpu.SemaphoreType.DMA((n,))
    mixed, grad_hidden, grad_down = pl.pallas_call(
        functools.partial(kernel, nd, ne, radix),
        out_shape=(jax.ShapeDtypeStruct((2 * tiles, 128), BF16), jax.ShapeDtypeStruct((2 * ne, units), BF16),
                   jax.ShapeDtypeStruct((units, 448), BF16)),
        in_specs=[vmem, vmem, vmem, pl.BlockSpec(memory_space=pl.ANY)],
        out_specs=(vmem, vmem, vmem),
        scratch_shapes=[
            pltpu.VMEM((2, units, width), BF16),
            pltpu.VMEM((8 * nd, 128), BF16),
            pltpu.VMEM((nd, 16, 128), F32),
            pltpu.VMEM((2 * ne, units), BF16),
            pltpu.VMEM((ne, 2, 128), F32),
            pltpu.VMEM((2 * ne, 128), F32),
            pltpu.VMEM((half + 1, 16 * nd, 128), BF16),
            pltpu.VMEM((toks * tiles, 128), F32),
            pltpu.VMEM((half + 1, 4 * tiles, 128), BF16),
            pltpu.VMEM((half, 4 * tiles, 128), BF16),
            pltpu.VMEM((4 * tiles, 128), F32),
            pltpu.VMEM((2 * tiles, 128), F32),
            pltpu.VMEM((nd, units, 2 * toks), BF16),
            pltpu.VMEM((nd, half, 16, 128), BF16),
            pltpu.VMEM((16 * half, 2 * units), F32),
            pltpu.VMEM((2 * ne, units), BF16),
            pltpu.VMEM((2 * ne, units), BF16),
            pltpu.VMEM((2 * units, 512), F32),
            pltpu.VMEM((units, 512), F32),
            dma(2), dma(6), dma(6), dma(radix), dma(radix), dma(ne // radix), dma(ne // radix),
            dma(half), dma(half), dma(half), dma(half), dma(nd), dma(nd), dma(nd), dma(nd),
        ],
        compiler_params=pltpu.CompilerParams(collective_id=0, has_side_effects=True,
                                             vmem_limit_bytes=48 * 1024 * 1024),
        cost_estimate=pl.CostEstimate(flops=6 * 2 * ne * units * width, bytes_accessed=2 * units * width,
                                      transcendentals=0),
    )(tokens, hidden, table, w_down)
    return (mixed.reshape(2, width), grad_hidden, grad_down)


def solution(mesh):
    return jax.shard_map(
        body,
        mesh=mesh,
        in_specs=(
            P("dp", "expert"),
            P(("dp", "expert"), None),
            P(("dp", "expert"), None),
            P(("dp", "expert"), None),
            P("expert", None),
        ),
        out_specs=(P(("dp", "expert"), None), P("dp", "expert"), P("expert", "dp")),
        check_vma=False,
    )
```

time: 676 us -> 131 us (0.19)
  waiting for transfers between devices: 568 us -> 0 us
  Pallas kernels: 0 us -> 121 us
  blocking collectives: 70.2 us -> 0 us
  between operations: 14.5 us -> 0.68 us
  matrix products: 10.3 us -> 0 us
    unnamed x4 -> x0, waiting for transfers between devices: 389 us -> none
    pallas_call x0 -> x1, Pallas kernels: none -> 121 us  [body(): pl.pallas_call(functools.partial(kernel, nd, ne, radix), out_shape=(jax.S...]
    reduce_scatter x1 -> x0, waiting for transfers between devices: 108 us -> none  [body(): lax.psum_scatter(term.astype(jnp.bfloat16), 'dp', scatter_dimension=1, ti...]
    all_gather x1 -> x0, waiting for transfers between devices: 70.9 us -> none  [body(): rows = lax.all_gather(cotangent, 'expert', axis=0, tiled=True)]
    all_gather x1 -> x0, blocking collectives: 70.2 us -> none  [body(): lax.all_gather(jnp.concatenate([named, weight], axis=1), 'expert', axis=0...]
    dot_general x3 -> x0, matrix products: 10.3 us -> none  [the longest x1 3.99 us: body(): jnp.dot(hw, w_down, preferred_element_type=jnp.float32).astype(jnp.bfloat16)]
  transfers between devices with their start and end apart: 3 -> 0, of which waited for: 3 -> 0; matrix products, arithmetic and copies ran while one was open for 3% -> 0% of each run, Pallas kernels for 0% -> 0%
where the time goes in v2:
time: 131 us; the launch traced here: 129 us
  Pallas kernels  121 us (92%)
  local copies, waits for them, and re-layouts  5.87 us (4%)
  other arithmetic  1.67 us (1%)
    pallas_call x1, Pallas kernels, body(): pl.pallas_call(functools.partial(kernel, nd, ne, radix), out_shape=(jax.S...  121 us
    unnamed x6, local copies, waits for them, and re-layouts  4.33 us

profile of v2, /device:TPU:1, one launch (start us, length us, event | category | flops | bytes accessed | tf_op | source)
XLA Modules:
  0.0 129.4 jit_solution(2346222364985415607)
XLA Ops:
  0.6 0.8 fusion
  1.4 0.1 pad.6.clone
  1.5 0.8 select_reduce_fusion
  2.3 0.1 fusion.3.tab_ref
  2.3 0.8 reshape.20
  3.3 0.0 copy-start
  3.3 2.0 %copy-done = bf16[256,7168]{1,0:T(8,128)(2,1)S(1)} copy-done((bf16[256,7168]{1,0:T(8,128)(2,1)S(1)}, bf16[256,7168]{1,0:T(8,128)(2,1)}, u32[]{:S(2)}) %copy-start) | copy-done | bytes 3670040
  5.3 0.0 copy-start.1
  5.3 0.8 copy-done.1
  6.1 121.2 %shard_map.76 = (bf16[112,128]{1,0:T(8,128)(2,1)S(1)}, bf16[128,256]{1,0:T(8,128)(2,1)S(1)}, bf16[256,448]{1,0:T(8,128)(2,1)S(1)}) custom-call(bf16[128,128]{1,0:T(8,128)(2,1)S(1)} %bitcast.8, bf16[128,256]{1,0:T(8,128)(2,1)S(1)} %copy-done.1, f32[2,128]{1,0:T(2,128)S(1)} %fusion.3.tab_ref, bf16[256,7168]{1,0:T(8,128)(2,1)S(1)} %copy-done), custom_call_target="tpu_custom_call" | custom-call | flops 1409286144 | bytes 3670016 | tf_op jit(solution)/shard_map/pallas_call | solution.py:347
  127.3 0.6 reshape.23
  127.9 0.8 copy.16
  128.8 0.6 copy.18
  (6 shorter events, 0.1 us)
Async XLA Ops:
  3.3 2.0 %copy-start = (bf16[256,7168]{1,0:T(8,128)(2,1)S(1)}, bf16[256,7168]{1,0:T(8,128)(2,1)}, u32[]{:S(2)}) copy-start(bf16[256,7168]{1,0:T(8,128)(2,1)} %w_ref.1) | copy-start | bytes 11010052
  5.3 0.8 copy-start.1

commit v3 on v1

v3 whole, which is shorter than its diff:
```python
import functools

import jax
import jax.numpy as jnp
from jax import lax
from jax.experimental import pallas as pl
from jax.experimental.pallas import tpu as pltpu
from jax.sharding import PartitionSpec as P

MESH = pl.DeviceIdType.MESH
F32, BF16 = jnp.float32, jnp.bfloat16
NT = (((1,), (1,)), ((), ()))
TN = (((0,), (0,)), ((), ()))
LAG = 4


def onehot(rows, columns, dtype):
    return (rows == columns).astype(F32).astype(dtype)


def kernel(nd, ne, leap, ids_ref, weight_ref, cot_ref, hid_ref, w_ref, mixed_ref, gh_ref, gd_ref,
           w2, ids, weights, cot, own_half, sib_half, own_hid, sib_hid, own_tab, sib_tab, table, flat, ring,
           y_buf, rs_in, rs_out, fin, mix_in, hw_t, blocks, g_acc, gh_send, gh_in, acc, acc_in,
           local_sem, sib_s, sib_r, tab_s, tab_r, ag_s, ag_r, rs_s, rs_r, hw_s, hw_r, bl_s, bl_r):
    nz, half = ne // 2, ne // 4
    toks = 4 * half
    reach = half // 2
    units = hid_ref.shape[1]
    tiles = w2.shape[2] // 128
    d, p = lax.axis_index("dp"), lax.axis_index("expert")
    z, c = p // 2, lax.rem(p, 2)
    way = 1 - 2 * c
    expert = p // 4
    base = 1 - c
    sibling = (d, p + 1 - 2 * c)

    def chip(steps):
        return (d, lax.rem(z + way * steps + 2 * nz, nz) * 2 + c)

    def copy(src, dst, send, recv, to):
        return pltpu.make_async_remote_copy(src_ref=src, dst_ref=dst, send_sem=send, recv_sem=recv,
                                            device_id=to, device_id_type=MESH)

    def each(low, high, step):
        def run(i, _):
            step(i)
            return 0
        lax.fori_loop(low, high, run, 0)

    loads = [pltpu.make_async_copy(a, b, local_sem.at[i]) for i, (a, b) in enumerate(
        ((ids_ref, ids), (weight_ref, weights), (cot_ref, cot), (hid_ref, own_hid), (w_ref, w2.at[0])))]
    for load in loads:
        load.start()

    barrier = pltpu.get_barrier_semaphore()

    def greet(to):
        pl.semaphore_signal(barrier, inc=1, device_id=to, device_id_type=MESH)

    greet(sibling)
    each(1, reach + 1, lambda i: greet(chip(-i)))
    greet(chip(-leap))
    greet(chip(1))
    greet(chip(leap))
    each(1, nd, lambda i: greet((lax.rem(d + i, nd), p)))

    loads[0].wait()
    loads[1].wait()
    lane = lax.broadcasted_iota(jnp.int32, (1, 128), 1)
    named = [jnp.zeros((1, 128), F32), jnp.zeros((1, 128), F32)]
    weight = [jnp.zeros((1, 128), F32), jnp.zeros((1, 128), F32)]
    for k in range(ids.shape[1]):
        for t in range(2):
            hit = ids[t:t + 1, k:k + 1] == (lane & 31)
            named[t] = jnp.where(hit, 1.0, named[t])
            weight[t] = jnp.where(hit, weights[t:t + 1, k:k + 1], weight[t])
    part = lane >> 5
    moved = jnp.where(named[0] > 0, 0.0, weight[1])
    kept = jnp.where(named[0] > 0, weight[1], 0.0)
    zero = jnp.zeros_like(moved)
    own_tab[0:1, :] = jnp.where(part == 0, weight[0], jnp.where(part == 2, moved, zero))
    own_tab[1:2, :] = jnp.where(part == 0, kept, jnp.where(part == 1, moved, zero))
    loads[2].wait()
    for block in range(nd):
        for q in range(4):
            tile = (block // 2) * 7 + 3 * (block % 2) + q
            own_half[pl.ds(8 * block + q, 2, stride=4), :] = cot[:, 128 * tile:128 * tile + 128].astype(F32)
    loads[3].wait()
    pl.semaphore_wait(barrier, 4 + reach + nd - 1)

    tab_copy = copy(own_tab, sib_tab, sib_s.at[6], sib_r.at[6], sibling)
    tok_copy = copy(own_half, sib_half, sib_s.at[0], sib_r.at[0], sibling)
    hid_copy = copy(own_hid, sib_hid, sib_s.at[1], sib_r.at[1], sibling)
    w_copy = copy(w_ref, w2.at[1], sib_s.at[2], sib_r.at[2], sibling)
    tab_copy.start()
    tok_copy.start()
    hid_copy.start()

    def tab(r, first):
        slot = first + r
        return copy(table.at[first], table.at[slot], tab_s.at[slot], tab_r.at[slot], chip(r))

    def ag(s):
        return copy(ring.at[s], ring.at[s + 1], ag_s.at[s], ag_r.at[s + 1], chip(1))

    ag_leap = copy(ring.at[0], ring.at[leap], ag_s.at[leap - 1], ag_r.at[leap], chip(leap))

    def ag_landed(s):
        copy(ring.at[0], ring.at[s], ag_s.at[0], ag_r.at[s], chip(1)).wait_recv()

    def near_step(s):
        ag_landed(s)
        ag(s).start()

    def far_step(s):
        ag_landed(s)
        if isinstance(s, int) and s == half - 1:
            @pl.when(c == 0)
            def _():
                ag(s).start()
        else:
            ag(s).start()

    def rounds(low, high):
        for s in range(low, high):
            if s < leap - 1:
                near_step(s)
            far = leap + s - late
            if leap <= far < half:
                far_step(far)

    tab_copy.wait_recv()
    mine, theirs = own_tab[...], sib_tab[...]
    first = c == 0
    table[0] = jnp.concatenate([jnp.where(first, mine, theirs), jnp.where(first, theirs, mine)], axis=0)
    each(0, reach, lambda i: tab(reach - i, 0).start())
    tok_copy.wait_recv()
    mine, theirs = own_half[...].reshape(nd, 8, 128), sib_half[...].reshape(nd, 8, 128)
    ring[0] = jnp.concatenate([jnp.where(first, mine, theirs), jnp.where(first, theirs, mine)],
                              axis=1).reshape(16 * nd, 128).astype(BF16)
    late = max(1, 2 * leap - 1 - half)
    ag(0).start()
    ag_leap.start()
    w_copy.start()
    top = max(leap - 1, half - leap + late)
    rounds(1, min(3, top))
    tab(reach, 0).wait_recv()
    each(0, reach, lambda i: tab(reach - i, reach).start())
    rounds(3, min(5, top))
    each(1, reach, lambda i: tab(i, 0).wait_recv())
    each(1, reach + 1, lambda i: tab(i, reach).wait_recv())
    hid_copy.wait_recv()

    for i in range(half):
        flat[4 * i:4 * i + 4, :] = table[base + i]
    row = lax.broadcasted_iota(jnp.int32, (toks, 4 * nz), 0)
    column = lax.broadcasted_iota(jnp.int32, (toks, 4 * nz), 1)

    def place_of(token):
        at = z - way * ((token >> 2) + base)
        at = jnp.where(at < 0, at + nz, at)
        at = jnp.where(at >= nz, at - nz, at)
        return at * 4 + (token & 3)

    place = place_of(row)
    picked = flat[...]
    lanes = lax.broadcasted_iota(jnp.int32, (toks, 128), 1)

    def coefficient(k):
        return jnp.sum(jnp.where(lanes == expert + 32 * k, picked, 0.0), axis=1, keepdims=True)

    keep, shift, give = coefficient(0), coefficient(1), coefficient(2)
    both = jnp.concatenate([own_hid[...], sib_hid[...]], axis=1)
    at = jnp.dot(onehot(place, column, BF16), both, preferred_element_type=F32)
    before = jnp.dot(onehot(place - 1, column, BF16), both, preferred_element_type=F32)
    hw = (keep * at + shift * before).astype(BF16)

    loads[4].wait()
    w_copy.wait_recv()

    def forward(m):
        at_column = pl.multiple_of(m * 896, 128)
        columns = w2[:, :, pl.ds(at_column, 896)].reshape(2 * units, 896)
        part = jnp.dot(hw, columns, preferred_element_type=F32)
        for k in range(7):
            y_buf[pl.ds(m * 7 + k, toks, stride=tiles), :] = part[:, 128 * k:128 * k + 128]

    each(0, nd // 2, forward)

    def y_at(s):
        return y_buf[pl.ds(pl.multiple_of((s - base) * 4 * tiles, 8), 4 * tiles), :]

    def rs(s):
        return copy(rs_out.at[s], rs_in.at[s - 1], rs_s.at[s], rs_r.at[s - 1], chip(-1))

    rs_leap = copy(rs_out.at[leap], rs_in.at[leap - 1], rs_s.at[leap], rs_r.at[leap - 1], chip(-leap))

    def rs_landed(s):
        copy(rs_out.at[0], rs_in.at[s], rs_s.at[0], rs_r.at[s], chip(-1)).wait_recv()

    def rs_add(s):
        rs_landed(s)
        rs_out[s] = (y_at(s) + rs_in[s].astype(F32)).astype(BF16)

    last = half - 1

    @pl.when(first)
    def _():
        rs_out[half] = y_at(half).astype(BF16)
        rs(half).start()

    rs_out[leap - 1] = y_at(leap - 1).astype(BF16)
    rs(leap - 1).start()
    rounds(5, min(6, top))

    spot_row = lax.broadcasted_iota(jnp.int32, (toks, 2 * toks), 0)
    spot_column = lax.broadcasted_iota(jnp.int32, (toks, 2 * toks), 1)
    turned = lax.dot_general(hw[:, :units], onehot(spot_row, spot_column, BF16), TN, preferred_element_type=F32)
    turned = turned + lax.dot_general(hw[:, units:], onehot(spot_row + toks, spot_column, BF16), TN,
                                      preferred_element_type=F32)
    hw_t[d] = turned.astype(BF16)

    def hw_copy(i, back):
        slot = lax.rem(d + nd - i, nd) if back else d
        return copy(hw_t.at[d], hw_t.at[slot], hw_s.at[i], hw_r.at[i], (lax.rem(d + i, nd), p))

    each(1, nd, lambda i: hw_copy(i, False).start())

    @pl.when(first)
    def _():
        rs_add(last)

    @pl.when(c == 1)
    def _():
        rs_out[last] = y_at(last).astype(BF16)

    def rs_send(s):
        if s == leap:
            rs_leap.start()
        else:
            rs(s).start()

    rs_send(last)
    far_left = list(range(last - 1, leap - 1, -1))
    near_left = list(range(leap - 2, 0, -1))
    order = []
    while far_left or near_left:
        if near_left:
            order.append(near_left.pop(0))
        if far_left:
            order.append(far_left.pop(0))

    def block_copy(i, back):
        to = lax.rem(d + i, nd)
        slot = lax.rem(d + nd - i, nd) if back else d
        return copy(ring.at[pl.ds(base, half), pl.ds(pl.multiple_of(16 * to, 16), 16), :], blocks.at[slot],
                    bl_s.at[i], bl_r.at[i], (to, p))

    own_block = pltpu.make_async_copy(
        ring.at[pl.ds(base, half), pl.ds(pl.multiple_of(16 * d, 16), 16), :], blocks.at[d], local_sem.at[5])
    quarter = lax.broadcasted_iota(jnp.int32, (16 * half, 128), 0) & 3

    def spread(values, low):
        return [jnp.where(quarter == k, values, jnp.zeros_like(values)) for k in range(low, 4)]

    g_acc[...] = jnp.zeros_like(g_acc)

    def backward(m):
        at_column = pl.multiple_of(m * 896, 128)
        columns = w2[:, :, pl.ds(at_column, 896)].reshape(2 * units, 896)
        even = ring[pl.ds(base, half), pl.ds(pl.multiple_of(32 * m, 16), 16), :].reshape(16 * half, 128)
        odd = ring[pl.ds(base, half), pl.ds(pl.multiple_of(32 * m + 16, 16), 16), :].reshape(16 * half, 128)
        wide = jnp.concatenate(spread(even, 0) + spread(odd, 1), axis=1)
        g_acc[...] += lax.dot_general(wide, columns, NT, preferred_element_type=F32)

    begun = 0
    going = 6
    gathered = False
    for count, s in enumerate(order):
        rs_add(s)
        rs_send(s)
        if count % 2 == 1 or count == len(order) - 1:
            if going < top:
                rounds(going, going + 1)
                going += 1
            elif not gathered:
                gathered = True

                @pl.when(first)
                def _():
                    ag_landed(half)

                if leap > 1:
                    ag_landed(leap - 1)
                each(1, nd, lambda i: block_copy(i, False).start())
                own_block.start()
        if gathered and begun < nd // 2:
            stop = min(begun + max(1, nd // 8), nd // 2)
            each(begun, stop, backward)
            begun = stop
    assert gathered
    each(begun, nd // 2, backward)

    fours = onehot(lax.broadcasted_iota(jnp.int32, (toks, 16 * half), 0),
                   lax.broadcasted_iota(jnp.int32, (toks, 16 * half), 1) >> 2, F32)
    back = jnp.dot(fours, g_acc[...], preferred_element_type=F32, precision=lax.Precision.HIGHEST)
    slots = (keep * back + give * pltpu.roll(back, toks - 1, 0)).astype(BF16)
    home = place_of(lax.broadcasted_iota(jnp.int32, (4 * nz, toks), 1))
    home_row = lax.broadcasted_iota(jnp.int32, (4 * nz, toks), 0)
    placed = jnp.dot(onehot(home, home_row, BF16), slots, preferred_element_type=F32).astype(BF16)
    gh_send[...] = placed[:, units:]
    gh_copy = copy(gh_send, gh_in, sib_s.at[4], sib_r.at[4], sibling)
    gh_copy.start()

    rs_landed(0)
    rs_landed(leap - 1)
    arrived = rs_in[0].astype(F32) + rs_in[leap - 1].astype(F32)

    @pl.when(first)
    def _():
        fin[...] = arrived

    @pl.when(c == 1)
    def _():
        fin[...] = arrived + y_at(0)

    mix_copy = copy(fin.at[pl.ds(pl.multiple_of(2 * tiles * (1 - c), 8), 2 * tiles)], mix_in,
                    sib_s.at[3], sib_r.at[3], sibling)
    mix_copy.start()

    repeat_row = lax.broadcasted_iota(jnp.int32, (2 * toks, 16 * half), 0)
    repeat_column = lax.broadcasted_iota(jnp.int32, (2 * toks, 16 * half), 1) >> 2
    repeat_own = onehot(repeat_row, repeat_column, BF16)
    repeat_sib = onehot(repeat_row, repeat_column + toks, BF16)

    def add_block(slot):
        left = jnp.concatenate([
            jnp.dot(hw_t[slot], repeat_own, preferred_element_type=F32),
            jnp.dot(hw_t[slot], repeat_sib, preferred_element_type=F32)], axis=0).astype(BF16)
        wide = jnp.concatenate(spread(blocks[slot].reshape(16 * half, 128), 0), axis=1)
        return jnp.dot(left, wide, preferred_element_type=F32)

    own_block.wait()
    acc[...] = add_block(d)

    def peer(i):
        hw_copy(i, True).wait_recv()
        block_copy(i, True).wait_recv()
        acc[...] += add_block(lax.rem(d + nd - i, nd))

    each(1, nd, peer)
    acc_copy = copy(acc.at[pl.ds(units, units)], acc_in, sib_s.at[5], sib_r.at[5], sibling)
    acc_copy.start()

    mix_copy.wait_recv()
    own_rows = fin[pl.ds(pl.multiple_of(2 * tiles * c, 8), 2 * tiles), :]
    mixed_ref[...] = (own_rows + mix_in[...]).astype(BF16)
    gh_copy.wait_recv()
    gh_ref[...] = (placed[:, :units].astype(F32) + gh_in[...].astype(F32)).astype(BF16)
    acc_copy.wait_recv()
    total = acc[pl.ds(0, units), :] + acc_in[...]
    gd_ref[...] = jnp.where(lax.rem(d, 2) == 1, total[:, 64:512], total[:, 0:448]).astype(BF16)

    for sent in (tab_copy, tok_copy, hid_copy, w_copy, mix_copy, gh_copy, acc_copy, ag_leap, rs_leap):
        sent.wait_send()
    each(1, reach + 1, lambda i: tab(i, 0).wait_send())
    each(1, reach + 1, lambda i: tab(i, reach).wait_send())
    each(0, leap - 1, lambda s: ag(s).wait_send())
    each(leap, last, lambda s: ag(s).wait_send())
    each(1, leap, lambda s: rs(s).wait_send())
    each(leap + 1, half, lambda s: rs(s).wait_send())

    @pl.when(first)
    def _():
        ag(last).wait_send()
        rs(half).wait_send()

    each(1, nd, lambda i: hw_copy(i, False).wait_send())
    each(1, nd, lambda i: block_copy(i, False).wait_send())


def body(hidden, expert_ids, route_weight, cotangent, w_down):
    width = cotangent.shape[1]
    units = hidden.shape[1]
    nd, ne = lax.axis_size("dp"), lax.axis_size("expert")
    half, tiles = ne // 4, width // 128
    leap = 5 * half // 8
    toks = 4 * half
    vmem = pl.BlockSpec(memory_space=pltpu.VMEM)
    anywhere = pl.BlockSpec(memory_space=pl.ANY)
    dma = lambda n: pltpu.SemaphoreType.DMA((n,))
    mixed, grad_hidden, grad_down = pl.pallas_call(
        functools.partial(kernel, nd, ne, leap),
        out_shape=(jax.ShapeDtypeStruct((2 * tiles, 128), BF16), jax.ShapeDtypeStruct((2 * ne, units), BF16),
                   jax.ShapeDtypeStruct((units, 448), BF16)),
        in_specs=[anywhere] * 5,
        out_specs=(vmem, vmem, vmem),
        scratch_shapes=[
            pltpu.VMEM((2, units, width), BF16),
            pltpu.VMEM(expert_ids.shape, jnp.int32),
            pltpu.VMEM(route_weight.shape, F32),
            pltpu.VMEM(cotangent.shape, BF16),
            pltpu.VMEM((8 * nd, 128), F32),
            pltpu.VMEM((8 * nd, 128), F32),
            pltpu.VMEM((2 * ne, units), BF16),
            pltpu.VMEM((2 * ne, units), BF16),
            pltpu.VMEM((2, 128), F32),
            pltpu.VMEM((2, 128), F32),
            pltpu.VMEM((half + 1, 4, 128), F32),
            pltpu.VMEM((toks, 128), F32),
            pltpu.VMEM((half + 1, 16 * nd, 128), BF16),
            pltpu.VMEM((toks * tiles, 128), F32),
            pltpu.VMEM((half, 4 * tiles, 128), BF16),
            pltpu.VMEM((half + 1, 4 * tiles, 128), BF16),
            pltpu.VMEM((4 * tiles, 128), F32),
            pltpu.VMEM((2 * tiles, 128), F32),
            pltpu.VMEM((nd, units, 2 * toks), BF16),
            pltpu.VMEM((nd, half, 16, 128), BF16),
            pltpu.VMEM((16 * half, 2 * units), F32),
            pltpu.VMEM((2 * ne, units), BF16),
            pltpu.VMEM((2 * ne, units), BF16),
            pltpu.VMEM((2 * units, 512), F32),
            pltpu.VMEM((units, 512), F32),
            dma(6), dma(7), dma(7), dma(half + 1), dma(half + 1), dma(half), dma(half + 1), dma(half + 1), dma(half),
            dma(nd), dma(nd), dma(nd), dma(nd),
        ],
        compiler_params=pltpu.CompilerParams(collective_id=0, has_side_effects=True,
                                             vmem_limit_bytes=56 * 1024 * 1024),
        cost_estimate=pl.CostEstimate(flops=12 * ne * units * width, bytes_accessed=2 * units * width,
                                      transcendentals=0),
    )(expert_ids, route_weight, cotangent, hidden, w_down)
    return (mixed.reshape(2, width), grad_hidden, grad_down)


def solution(mesh):
    return jax.shard_map(
        body,
        mesh=mesh,
        in_specs=(
            P("dp", "expert"),
            P(("dp", "expert"), None),
            P(("dp", "expert"), None),
            P(("dp", "expert"), None),
            P("expert", None),
        ),
        out_specs=(P(("dp", "expert"), None), P("dp", "expert"), P("expert", "dp")),
        check_vma=False,
    )
```

time: 676 us -> 108 us (0.16)
  waiting for transfers between devices: 568 us -> 0 us
  Pallas kernels: 0 us -> 100 us
  blocking collectives: 70.2 us -> 0 us
  between operations: 14.5 us -> 0.64 us
  matrix products: 10.3 us -> 0 us
    unnamed x4 -> x0, waiting for transfers between devices: 389 us -> none
    reduce_scatter x1 -> x0, waiting for transfers between devices: 108 us -> none  [body(): lax.psum_scatter(term.astype(jnp.bfloat16), 'dp', scatter_dimension=1, ti...]
    pallas_call x0 -> x1, Pallas kernels: none -> 100 us  [body(): pl.pallas_call(functools.partial(kernel, nd, ne, leap), out_shape=(jax.Sh...]
    all_gather x1 -> x0, waiting for transfers between devices: 70.9 us -> none  [body(): rows = lax.all_gather(cotangent, 'expert', axis=0, tiled=True)]
    all_gather x1 -> x0, blocking collectives: 70.2 us -> none  [body(): lax.all_gather(jnp.concatenate([named, weight], axis=1), 'expert', axis=0...]
    dot_general x3 -> x0, matrix products: 10.3 us -> none  [the longest x1 3.99 us: body(): jnp.dot(hw, w_down, preferred_element_type=jnp.float32).astype(jnp.bfloat16)]
  transfers between devices with their start and end apart: 3 -> 0, of which waited for: 3 -> 0; matrix products, arithmetic and copies ran while one was open for 3% -> 0% of each run, Pallas kernels for 0% -> 0%
where the time goes in v3:
time: 108 us; the launch traced here: 106 us
  Pallas kernels  100 us (93%)
  local copies, waits for them, and re-layouts  4.62 us (4%)
    pallas_call x1, Pallas kernels, body(): pl.pallas_call(functools.partial(kernel, nd, ne, leap), out_shape=(jax.Sh...  100 us
    unnamed x2, local copies, waits for them, and re-layouts  3.25 us

profile of v3, /device:TPU:1, one launch (start us, length us, event | category | flops | bytes accessed | tf_op | source)
XLA Modules:
  0.0 105.8 jit_solution(15180441202978740911)
XLA Ops:
  0.6 100.5 %shard_map.76 = (bf16[112,128]{1,0:T(8,128)(2,1)}, bf16[128,256]{1,0:T(8,128)(2,1)}, bf16[256,448]{1,0:T(8,128)(2,1)}) custom-call(s32[2,8]{1,0:T(2,128)} %ids_ref.1, f32[2,8]{1,0:T(2,128)} %weight_ref.1, bf16[2,7168]{1,0:T(2,128)(2,1)} %cot_ref.1, bf16[128,256]{1,0:T(8,128)(2,1)} %hid_ref.1, bf16[256,7168]{1,0:T(8,128)(2,1)} %w_ref.1), custom_call_target="tpu_custom_call" | custom-call | flops 1409286144 | bytes 3670016 | tf_op jit(solution)/shard_map/pallas_call | solution.py:392
  101.1 1.4 %reshape.9 = bf16[2,7168]{1,0:T(2,128)(2,1)} reshape(bf16[112,128]{1,0:T(8,128)(2,1)} %get-tuple-element.6) | data formatting | bytes 57344 | tf_op jit(solution)/shard_map/reshape | solution.py:432
  102.5 1.8 %copy.8 = bf16[256,448]{0,1:T(8,128)(2,1)} copy(bf16[256,448]{1,0:T(8,128)(2,1)} %get-tuple-element.11) | data formatting | bytes 458752
  104.3 1.5 %copy.10 = bf16[128,256]{1,0:T(8,128)(2,1)} copy(bf16[128,256]{1,0:T(8,128)(2,1)} %get-tuple-element.16) | data formatting | bytes 131072

commit v4 on v3

--- a/solution.py
+++ b/solution.py
@@ -20,7 +20,7 @@
 
 def kernel(nd, ne, leap, ids_ref, weight_ref, cot_ref, hid_ref, w_ref, mixed_ref, gh_ref, gd_ref,
            w2, ids, weights, cot, own_half, sib_half, own_hid, sib_hid, own_tab, sib_tab, table, flat, ring,
-           y_buf, rs_in, rs_out, fin, mix_in, hw_t, blocks, g_acc, gh_send, gh_in, acc, acc_in,
+           y_buf, rs_in, rs_out, fin, mix_in, hw_t, lefts, blocks, g_acc, gh_send, gh_in, acc, acc_in,
            local_sem, sib_s, sib_r, tab_s, tab_r, ag_s, ag_r, rs_s, rs_r, hw_s, hw_r, bl_s, bl_r):
     nz, half = ne // 2, ne // 4
     toks = 4 * half
@@ -80,21 +80,19 @@
     zero = jnp.zeros_like(moved)
     own_tab[0:1, :] = jnp.where(part == 0, weight[0], jnp.where(part == 2, moved, zero))
     own_tab[1:2, :] = jnp.where(part == 0, kept, jnp.where(part == 1, moved, zero))
+    pl.semaphore_wait(barrier, 4 + reach + nd - 1)
+
+    tab_copy = copy(own_tab, sib_tab, sib_s.at[6], sib_r.at[6], sibling)
+    tok_copy = copy(own_half, sib_half, sib_s.at[0], sib_r.at[0], sibling)
+    hid_copy = copy(own_hid, sib_hid, sib_s.at[1], sib_r.at[1], sibling)
+    w_copy = copy(w_ref, w2.at[1], sib_s.at[2], sib_r.at[2], sibling)
+    tab_copy.start()
     loads[2].wait()
     for block in range(nd):
         for q in range(4):
             tile = (block // 2) * 7 + 3 * (block % 2) + q
             own_half[pl.ds(8 * block + q, 2, stride=4), :] = cot[:, 128 * tile:128 * tile + 128].astype(F32)
-    loads[3].wait()
-    pl.semaphore_wait(barrier, 4 + reach + nd - 1)
-
-    tab_copy = copy(own_tab, sib_tab, sib_s.at[6], sib_r.at[6], sibling)
-    tok_copy = copy(own_half, sib_half, sib_s.at[0], sib_r.at[0], sibling)
-    hid_copy = copy(own_hid, sib_hid, sib_s.at[1], sib_r.at[1], sibling)
-    w_copy = copy(w_ref, w2.at[1], sib_s.at[2], sib_r.at[2], sibling)
-    tab_copy.start()
     tok_copy.start()
-    hid_copy.start()
 
     def tab(r, first):
         slot = first + r
@@ -134,6 +132,8 @@
     first = c == 0
     table[0] = jnp.concatenate([jnp.where(first, mine, theirs), jnp.where(first, theirs, mine)], axis=0)
     each(0, reach, lambda i: tab(reach - i, 0).start())
+    loads[3].wait()
+    hid_copy.start()
     tok_copy.wait_recv()
     mine, theirs = own_half[...].reshape(nd, 8, 128), sib_half[...].reshape(nd, 8, 128)
     ring[0] = jnp.concatenate([jnp.where(first, mine, theirs), jnp.where(first, theirs, mine)],
@@ -143,10 +143,10 @@
     ag_leap.start()
     w_copy.start()
     top = max(leap - 1, half - leap + late)
-    rounds(1, min(3, top))
+    rounds(1, min(2, top))
     tab(reach, 0).wait_recv()
     each(0, reach, lambda i: tab(reach - i, reach).start())
-    rounds(3, min(5, top))
+    rounds(2, min(4, top))
     each(1, reach, lambda i: tab(i, 0).wait_recv())
     each(1, reach + 1, lambda i: tab(i, reach).wait_recv())
     hid_copy.wait_recv()
@@ -211,7 +211,7 @@
 
     rs_out[leap - 1] = y_at(leap - 1).astype(BF16)
     rs(leap - 1).start()
-    rounds(5, min(6, top))
+    rounds(4, min(6, top))
 
     spot_row = lax.broadcasted_iota(jnp.int32, (toks, 2 * toks), 0)
     spot_column = lax.broadcasted_iota(jnp.int32, (toks, 2 * toks), 1)
@@ -272,6 +272,20 @@
         odd = ring[pl.ds(base, half), pl.ds(pl.multiple_of(32 * m + 16, 16), 16), :].reshape(16 * half, 128)
         wide = jnp.concatenate(spread(even, 0) + spread(odd, 1), axis=1)
         g_acc[...] += lax.dot_general(wide, columns, NT, preferred_element_type=F32)
+
+    repeat_row = lax.broadcasted_iota(jnp.int32, (2 * toks, 16 * half), 0)
+    repeat_column = lax.broadcasted_iota(jnp.int32, (2 * toks, 16 * half), 1) >> 2
+    repeat_own = onehot(repeat_row, repeat_column, BF16)
+    repeat_sib = onehot(repeat_row, repeat_column + toks, BF16)
+
+    def make_left(slot):
+        lefts[slot] = jnp.concatenate([
+            jnp.dot(hw_t[slot], repeat_own, preferred_element_type=F32),
+            jnp.dot(hw_t[slot], repeat_sib, preferred_element_type=F32)], axis=0).astype(BF16)
+
+    def peer_left(i):
+        hw_copy(i, True).wait_recv()
+        make_left(lax.rem(d + nd - i, nd))
 
     begun = 0
     going = 6
@@ -298,6 +312,14 @@
             stop = min(begun + max(1, nd // 8), nd // 2)
             each(begun, stop, backward)
             begun = stop
+        if count == len(order) - 2:
+            make_left(d)
+            each(1, nd // 2, peer_left)
+        if count == len(order) - 1:
+            if len(order) < 2:
+                make_left(d)
+                each(1, nd // 2, peer_left)
+            each(nd // 2, nd, peer_left)
     assert gathered
     each(begun, nd // 2, backward)
 
@@ -312,6 +334,21 @@
     gh_copy = copy(gh_send, gh_in, sib_s.at[4], sib_r.at[4], sibling)
     gh_copy.start()
 
+    def add_block(slot):
+        wide = jnp.concatenate(spread(blocks[slot].reshape(16 * half, 128), 0), axis=1)
+        return jnp.dot(lefts[slot], wide, preferred_element_type=F32)
+
+    own_block.wait()
+    acc[...] = add_block(d)
+
+    def peer(i):
+        block_copy(i, True).wait_recv()
+        acc[...] += add_block(lax.rem(d + nd - i, nd))
+
+    each(1, nd, peer)
+    acc_copy = copy(acc.at[pl.ds(units, units)], acc_in, sib_s.at[5], sib_r.at[5], sibling)
+    acc_copy.start()
+
     rs_landed(0)
     rs_landed(leap - 1)
     arrived = rs_in[0].astype(F32) + rs_in[leap - 1].astype(F32)
@@ -327,30 +364,6 @@
     mix_copy = copy(fin.at[pl.ds(pl.multiple_of(2 * tiles * (1 - c), 8), 2 * tiles)], mix_in,
                     sib_s.at[3], sib_r.at[3], sibling)
     mix_copy.start()
-
-    repeat_row = lax.broadcasted_iota(jnp.int32, (2 * toks, 16 * half), 0)
-    repeat_column = lax.broadcasted_iota(jnp.int32, (2 * toks, 16 * half), 1) >> 2
-    repeat_own = onehot(repeat_row, repeat_column, BF16)
-    repeat_sib = onehot(repeat_row, repeat_column + toks, BF16)
-
-    def add_block(slot):
-        left = jnp.concatenate([
-            jnp.dot(hw_t[slot], repeat_own, preferred_element_type=F32),
-            jnp.dot(hw_t[slot], repeat_sib, preferred_element_type=F32)], axis=0).astype(BF16)
-        wide = jnp.concatenate(spread(blocks[slot].reshape(16 * half, 128), 0), axis=1)
-        return jnp.dot(left, wide, preferred_element_type=F32)
-
-    own_block.wait()
-    acc[...] = add_block(d)
-
-    def peer(i):
-        hw_copy(i, True).wait_recv()
-        block_copy(i, True).wait_recv()
-        acc[...] += add_block(lax.rem(d + nd - i, nd))
-
-    each(1, nd, peer)
-    acc_copy = copy(acc.at[pl.ds(units, units)], acc_in, sib_s.at[5], sib_r.at[5], sibling)
-    acc_copy.start()
 
     mix_copy.wait_recv()
     own_rows = fin[pl.ds(pl.multiple_of(2 * tiles * c, 8), 2 * tiles), :]
@@ -415,6 +428,7 @@
             pltpu.VMEM((4 * tiles, 128), F32),
             pltpu.VMEM((2 * tiles, 128), F32),
             pltpu.VMEM((nd, units, 2 * toks), BF16),
+            pltpu.VMEM((nd, 2 * units, 16 * half), BF16),
             pltpu.VMEM((nd, half, 16, 128), BF16),
             pltpu.VMEM((16 * half, 2 * units), F32),
             pltpu.VMEM((2 * ne, units), BF16),

time: 108 us -> 101 us (0.935)
  the two profiles are of different devices: /device:TPU:1 before, /device:TPU:97 now
where the time goes in v4:
time: 101 us; the launch traced here: 100 us
  Pallas kernels  95 us (94%)
  local copies, waits for them, and re-layouts  4.62 us (5%)
    pallas_call x1, Pallas kernels, body(): pl.pallas_call(functools.partial(kernel, nd, ne, leap), out_shape=(jax.Sh...  95 us
    unnamed x2, local copies, waits for them, and re-layouts  3.25 us

profile of v4, /device:TPU:97, one launch (start us, length us, event | category | flops | bytes accessed | tf_op | source)
XLA Modules:
  0.0 100.3 jit_solution(4603638089325120238)
XLA Ops:
  0.6 95.0 %shard_map.76 = (bf16[112,128]{1,0:T(8,128)(2,1)}, bf16[128,256]{1,0:T(8,128)(2,1)}, bf16[256,448]{1,0:T(8,128)(2,1)}) custom-call(s32[2,8]{1,0:T(2,128)} %ids_ref.1, f32[2,8]{1,0:T(2,128)} %weight_ref.1, bf16[2,7168]{1,0:T(2,128)(2,1)} %cot_ref.1, bf16[128,256]{1,0:T(8,128)(2,1)} %hid_ref.1, bf16[256,7168]{1,0:T(8,128)(2,1)} %w_ref.1), custom_call_target="tpu_custom_call" | custom-call | flops 1409286144 | bytes 3670016 | tf_op jit(solution)/shard_map/pallas_call | solution.py:405
  95.7 1.4 %reshape.9 = bf16[2,7168]{1,0:T(2,128)(2,1)} reshape(bf16[112,128]{1,0:T(8,128)(2,1)} %get-tuple-element.6) | data formatting | bytes 57344 | tf_op jit(solution)/shard_map/reshape | solution.py:446
  97.0 1.8 %copy.8 = bf16[256,448]{0,1:T(8,128)(2,1)} copy(bf16[256,448]{1,0:T(8,128)(2,1)} %get-tuple-element.11) | data formatting | bytes 458752
  98.8 1.5 %copy.10 = bf16[128,256]{1,0:T(8,128)(2,1)} copy(bf16[128,256]{1,0:T(8,128)(2,1)} %get-tuple-element.16) | data formatting | bytes 131072

commit v5 on v4

--- a/solution.py
+++ b/solution.py
@@ -18,7 +18,7 @@
     return (rows == columns).astype(F32).astype(dtype)
 
 
-def kernel(nd, ne, leap, ids_ref, weight_ref, cot_ref, hid_ref, w_ref, mixed_ref, gh_ref, gd_ref,
+def kernel(nd, ne, leap, back_leap, cuts, back_cuts, ids_ref, weight_ref, cot_ref, hid_ref, w_ref, mixed_ref, gh_ref, gd_ref,
            w2, ids, weights, cot, own_half, sib_half, own_hid, sib_hid, own_tab, sib_tab, table, flat, ring,
            y_buf, rs_in, rs_out, fin, mix_in, hw_t, lefts, blocks, g_acc, gh_send, gh_in, acc, acc_in,
            local_sem, sib_s, sib_r, tab_s, tab_r, ag_s, ag_r, rs_s, rs_r, hw_s, hw_r, bl_s, bl_r):
@@ -61,7 +61,7 @@
     each(1, reach + 1, lambda i: greet(chip(-i)))
     greet(chip(-leap))
     greet(chip(1))
-    greet(chip(leap))
+    greet(chip(back_leap))
     each(1, nd, lambda i: greet((lax.rem(d + i, nd), p)))
 
     loads[0].wait()
@@ -98,26 +98,32 @@
         slot = first + r
         return copy(table.at[first], table.at[slot], tab_s.at[slot], tab_r.at[slot], chip(r))
 
-    def ag(s):
-        return copy(ring.at[s], ring.at[s + 1], ag_s.at[s], ag_r.at[s + 1], chip(1))
-
-    ag_leap = copy(ring.at[0], ring.at[leap], ag_s.at[leap - 1], ag_r.at[leap], chip(leap))
-
-    def ag_landed(s):
-        copy(ring.at[0], ring.at[s], ag_s.at[0], ag_r.at[s], chip(1)).wait_recv()
+    def ag_copy(source, target, h, send, steps):
+        rows = pl.ds(h * (16 * nd // cuts), 16 * nd // cuts)
+        return copy(ring.at[source, rows], ring.at[target, rows], ag_s.at[send * cuts + h], ag_r.at[target * cuts + h],
+                    chip(steps))
+
+    def ag(s, h):
+        return ag_copy(s, s + 1, h, s, 1)
+
+    def ag_leap(h):
+        return ag_copy(0, leap, h, leap - 1, leap)
+
+    def ag_landed(s, h):
+        ag_copy(0, s, h, 0, 1).wait_recv()
 
     def near_step(s):
-        ag_landed(s)
-        ag(s).start()
+        for h in range(cuts):
+            ag_landed(s, h)
+            ag(s, h).start()
 
     def far_step(s):
-        ag_landed(s)
-        if isinstance(s, int) and s == half - 1:
-            @pl.when(c == 0)
-            def _():
-                ag(s).start()
-        else:
-            ag(s).start()
+        for h in range(cuts):
+            ag_landed(s, h)
+            if s == half - 1:
+                pl.when(c == 0)(ag(s, h).start)
+            else:
+                ag(s, h).start()
 
     def rounds(low, high):
         for s in range(low, high):
@@ -139,8 +145,10 @@
     ring[0] = jnp.concatenate([jnp.where(first, mine, theirs), jnp.where(first, theirs, mine)],
                               axis=1).reshape(16 * nd, 128).astype(BF16)
     late = max(1, 2 * leap - 1 - half)
-    ag(0).start()
-    ag_leap.start()
+    for h in range(cuts):
+        ag(0, h).start()
+    for h in range(cuts):
+        ag_leap(h).start()
     w_copy.start()
     top = max(leap - 1, half - leap + late)
     rounds(1, min(2, top))
@@ -187,30 +195,47 @@
 
     each(0, nd // 2, forward)
 
-    def y_at(s):
-        return y_buf[pl.ds(pl.multiple_of((s - base) * 4 * tiles, 8), 4 * tiles), :]
-
-    def rs(s):
-        return copy(rs_out.at[s], rs_in.at[s - 1], rs_s.at[s], rs_r.at[s - 1], chip(-1))
-
-    rs_leap = copy(rs_out.at[leap], rs_in.at[leap - 1], rs_s.at[leap], rs_r.at[leap - 1], chip(-leap))
-
-    def rs_landed(s):
-        copy(rs_out.at[0], rs_in.at[s], rs_s.at[0], rs_r.at[s], chip(-1)).wait_recv()
-
-    def rs_add(s):
-        rs_landed(s)
-        rs_out[s] = (y_at(s) + rs_in[s].astype(F32)).astype(BF16)
+    piece = 4 * tiles // back_cuts
+
+    def y_at(s, h):
+        return y_buf[pl.ds(pl.multiple_of((s - base) * 4 * tiles + h * piece, 8), piece), :]
+
+    def rs_copy(source, target, h, steps):
+        rows = pl.ds(h * piece, piece)
+        return copy(rs_out.at[source, rows], rs_in.at[target, rows], rs_s.at[source * back_cuts + h],
+                    rs_r.at[target * back_cuts + h], chip(-steps))
+
+    def rs(s, h):
+        return rs_copy(s, s - 1, h, 1)
+
+    def rs_send(s, h):
+        if s == back_leap:
+            rs_copy(s, s - 1, h, s).start()
+        else:
+            rs(s, h).start()
+
+    def rs_landed(s, h):
+        rs_copy(1, s, h, 1).wait_recv()
+
+    def rs_begin(s, h):
+        rs_out[s, pl.ds(h * piece, piece), :] = y_at(s, h).astype(BF16)
+
+    def rs_add(s, h):
+        rs_landed(s, h)
+        rs_out[s, pl.ds(h * piece, piece), :] = (
+            y_at(s, h) + rs_in[s, pl.ds(h * piece, piece), :].astype(F32)).astype(BF16)
 
     last = half - 1
 
     @pl.when(first)
     def _():
-        rs_out[half] = y_at(half).astype(BF16)
-        rs(half).start()
-
-    rs_out[leap - 1] = y_at(leap - 1).astype(BF16)
-    rs(leap - 1).start()
+        for h in range(back_cuts):
+            rs_begin(half, h)
+            rs_send(half, h)
+
+    for h in range(back_cuts):
+        rs_begin(back_leap - 1, h)
+        rs_send(back_leap - 1, h)
     rounds(4, min(6, top))
 
     spot_row = lax.broadcasted_iota(jnp.int32, (toks, 2 * toks), 0)
@@ -226,23 +251,13 @@
 
     each(1, nd, lambda i: hw_copy(i, False).start())
 
-    @pl.when(first)
-    def _():
-        rs_add(last)
-
-    @pl.when(c == 1)
-    def _():
-        rs_out[last] = y_at(last).astype(BF16)
-
-    def rs_send(s):
-        if s == leap:
-            rs_leap.start()
-        else:
-            rs(s).start()
-
-    rs_send(last)
-    far_left = list(range(last - 1, leap - 1, -1))
-    near_left = list(range(leap - 2, 0, -1))
+    for h in range(back_cuts):
+        pl.when(first)(functools.partial(rs_add, last, h))
+        pl.when(c == 1)(functools.partial(rs_begin, last, h))
+        rs_send(last, h)
+
+    far_left = list(range(last - 1, back_leap - 1, -1))
+    near_left = list(range(back_leap - 2, 0, -1))
     order = []
     while far_left or near_left:
         if near_left:
@@ -291,8 +306,9 @@
     going = 6
     gathered = False
     for count, s in enumerate(order):
-        rs_add(s)
-        rs_send(s)
+        for h in range(back_cuts):
+            rs_add(s, h)
+            rs_send(s, h)
         if count % 2 == 1 or count == len(order) - 1:
             if going < top:
                 rounds(going, going + 1)
@@ -300,12 +316,9 @@
             elif not gathered:
                 gathered = True
 
-                @pl.when(first)
-                def _():
-                    ag_landed(half)
-
-                if leap > 1:
-                    ag_landed(leap - 1)
+                for h in range(cuts):
+                    pl.when(first)(functools.partial(ag_landed, half, h))
+                    ag_landed(leap - 1, h)
                 each(1, nd, lambda i: block_copy(i, False).start())
                 own_block.start()
         if gathered and begun < nd // 2:
@@ -349,9 +362,11 @@
     acc_copy = copy(acc.at[pl.ds(units, units)], acc_in, sib_s.at[5], sib_r.at[5], sibling)
     acc_copy.start()
 
-    rs_landed(0)
-    rs_landed(leap - 1)
-    arrived = rs_in[0].astype(F32) + rs_in[leap - 1].astype(F32)
+    for h in range(back_cuts):
+        rs_landed(back_leap - 1, h)
+    for h in range(back_cuts):
+        rs_landed(0, h)
+    arrived = rs_in[0].astype(F32) + rs_in[back_leap - 1].astype(F32)
 
     @pl.when(first)
     def _():
@@ -359,7 +374,7 @@
 
     @pl.when(c == 1)
     def _():
-        fin[...] = arrived + y_at(0)
+        fin[...] = arrived + y_buf[pl.ds(0, 4 * tiles), :]
 
     mix_copy = copy(fin.at[pl.ds(pl.multiple_of(2 * tiles * (1 - c), 8), 2 * tiles)], mix_in,
                     sib_s.at[3], sib_r.at[3], sibling)
@@ -374,20 +389,18 @@
     total = acc[pl.ds(0, units), :] + acc_in[...]
     gd_ref[...] = jnp.where(lax.rem(d, 2) == 1, total[:, 64:512], total[:, 0:448]).astype(BF16)
 
-    for sent in (tab_copy, tok_copy, hid_copy, w_copy, mix_copy, gh_copy, acc_copy, ag_leap, rs_leap):
+    for sent in (tab_copy, tok_copy, hid_copy, w_copy, mix_copy, gh_copy, acc_copy):
         sent.wait_send()
     each(1, reach + 1, lambda i: tab(i, 0).wait_send())
     each(1, reach + 1, lambda i: tab(i, reach).wait_send())
-    each(0, leap - 1, lambda s: ag(s).wait_send())
-    each(leap, last, lambda s: ag(s).wait_send())
-    each(1, leap, lambda s: rs(s).wait_send())
-    each(leap + 1, half, lambda s: rs(s).wait_send())
-
-    @pl.when(first)
-    def _():
-        ag(last).wait_send()
-        rs(half).wait_send()
-
+    for h in range(cuts):
+        ag_leap(h).wait_send()
+        each(0, leap - 1, lambda s: ag(s, h).wait_send())
+        each(leap, last, lambda s: ag(s, h).wait_send())
+        pl.when(first)(ag(last, h).wait_send)
+    for h in range(back_cuts):
+        each(1, half, lambda s: rs(s, h).wait_send())
+        pl.when(first)(rs(half, h).wait_send)
     each(1, nd, lambda i: hw_copy(i, False).wait_send())
     each(1, nd, lambda i: block_copy(i, False).wait_send())
 
@@ -398,12 +411,13 @@
     nd, ne = lax.axis_size("dp"), lax.axis_size("expert")
     half, tiles = ne // 4, width // 128
     leap = 5 * half // 8
+    back_leap, cuts, back_cuts = leap - half // 16, 2, 1
     toks = 4 * half
     vmem = pl.BlockSpec(memory_space=pltpu.VMEM)
     anywhere = pl.BlockSpec(memory_space=pl.ANY)
     dma = lambda n: pltpu.SemaphoreType.DMA((n,))
     mixed, grad_hidden, grad_down = pl.pallas_call(
-        functools.partial(kernel, nd, ne, leap),
+        functools.partial(kernel, nd, ne, leap, back_leap, cuts, back_cuts),
         out_shape=(jax.ShapeDtypeStruct((2 * tiles, 128), BF16), jax.ShapeDtypeStruct((2 * ne, units), BF16),
                    jax.ShapeDtypeStruct((units, 448), BF16)),
         in_specs=[anywhere] * 5,
@@ -435,7 +449,7 @@
             pltpu.VMEM((2 * ne, units), BF16),
             pltpu.VMEM((2 * units, 512), F32),
             pltpu.VMEM((units, 512), F32),
-            dma(6), dma(7), dma(7), dma(half + 1), dma(half + 1), dma(half), dma(half + 1), dma(half + 1), dma(half),
+            dma(6), dma(7), dma(7), dma(half + 1), dma(half + 1), dma(cuts * half), dma(cuts * (half + 1)), dma(back_cuts * (half + 1)), dma(back_cuts * half),
             dma(nd), dma(nd), dma(nd), dma(nd),
         ],
         compiler_params=pltpu.CompilerParams(collective_id=0, has_side_effects=True,

time: 101 us -> 92.3 us (0.914)
  the two profiles are of different devices: /device:TPU:97 before, /device:TPU:1 now
where the time goes in v5:
time: 92.3 us; the launch traced here: 92 us
  Pallas kernels  86.8 us (94%)
  local copies, waits for them, and re-layouts  4.62 us (5%)
    pallas_call x1, Pallas kernels, body(): pl.pallas_call(functools.partial(kernel, nd, ne, leap, back_leap, cuts, b...  86.8 us
    unnamed x2, local copies, waits for them, and re-layouts  3.25 us

profile of v5, /device:TPU:1, one launch (start us, length us, event | category | flops | bytes accessed | tf_op | source)
XLA Modules:
  0.0 92.0 jit_solution(13400043949059695993)
XLA Ops:
  0.6 86.8 %shard_map.76 = (bf16[112,128]{1,0:T(8,128)(2,1)}, bf16[128,256]{1,0:T(8,128)(2,1)}, bf16[256,448]{1,0:T(8,128)(2,1)}) custom-call(s32[2,8]{1,0:T(2,128)} %ids_ref.1, f32[2,8]{1,0:T(2,128)} %weight_ref.1, bf16[2,7168]{1,0:T(2,128)(2,1)} %cot_ref.1, bf16[128,256]{1,0:T(8,128)(2,1)} %hid_ref.1, bf16[256,7168]{1,0:T(8,128)(2,1)} %w_ref.1), custom_call_target="tpu_custom_call" | custom-call | flops 1409286144 | bytes 3670016 | tf_op jit(solution)/shard_map/pallas_call | solution.py:419
  87.4 1.4 %reshape.9 = bf16[2,7168]{1,0:T(2,128)(2,1)} reshape(bf16[112,128]{1,0:T(8,128)(2,1)} %get-tuple-element.6) | data formatting | bytes 57344 | tf_op jit(solution)/shard_map/reshape | solution.py:460
  88.8 1.8 %copy.8 = bf16[256,448]{0,1:T(8,128)(2,1)} copy(bf16[256,448]{1,0:T(8,128)(2,1)} %get-tuple-element.11) | data formatting | bytes 458752
  90.5 1.5 %copy.10 = bf16[128,256]{1,0:T(8,128)(2,1)} copy(bf16[128,256]{1,0:T(8,128)(2,1)} %get-tuple-element.16) | data formatting | bytes 131072

commit v6 on v5

--- a/solution.py
+++ b/solution.py
@@ -411,7 +411,7 @@
     nd, ne = lax.axis_size("dp"), lax.axis_size("expert")
     half, tiles = ne // 4, width // 128
     leap = 5 * half // 8
-    back_leap, cuts, back_cuts = leap - half // 16, 2, 1
+    back_leap, cuts, back_cuts = leap - half // 16, 2, 2
     toks = 4 * half
     vmem = pl.BlockSpec(memory_space=pltpu.VMEM)
     anywhere = pl.BlockSpec(memory_space=pl.ANY)

time: 92.3 us -> 91.8 us (level)
  no operation moved by 1% of the time
where the time goes in v6:
time: 91.8 us; the launch traced here: 91.5 us
  Pallas kernels  86.2 us (94%)
  local copies, waits for them, and re-layouts  4.62 us (5%)
    pallas_call x1, Pallas kernels, body(): pl.pallas_call(functools.partial(kernel, nd, ne, leap, back_leap, cuts, b...  86.2 us
    unnamed x2, local copies, waits for them, and re-layouts  3.25 us

profile of v6, /device:TPU:1, one launch (start us, length us, event | category | flops | bytes accessed | tf_op | source)
XLA Modules:
  0.0 91.5 jit_solution(12066423753869723380)
XLA Ops:
  0.6 86.2 %shard_map.76 = (bf16[112,128]{1,0:T(8,128)(2,1)}, bf16[128,256]{1,0:T(8,128)(2,1)}, bf16[256,448]{1,0:T(8,128)(2,1)}) custom-call(s32[2,8]{1,0:T(2,128)} %ids_ref.1, f32[2,8]{1,0:T(2,128)} %weight_ref.1, bf16[2,7168]{1,0:T(2,128)(2,1)} %cot_ref.1, bf16[128,256]{1,0:T(8,128)(2,1)} %hid_ref.1, bf16[256,7168]{1,0:T(8,128)(2,1)} %w_ref.1), custom_call_target="tpu_custom_call" | custom-call | flops 1409286144 | bytes 3670016 | tf_op jit(solution)/shard_map/pallas_call | solution.py:419
  86.9 1.4 %reshape.9 = bf16[2,7168]{1,0:T(2,128)(2,1)} reshape(bf16[112,128]{1,0:T(8,128)(2,1)} %get-tuple-element.6) | data formatting | bytes 57344 | tf_op jit(solution)/shard_map/reshape | solution.py:460
  88.2 1.8 %copy.8 = bf16[256,448]{0,1:T(8,128)(2,1)} copy(bf16[256,448]{1,0:T(8,128)(2,1)} %get-tuple-element.11) | data formatting | bytes 458752
  90.0 1.5 %copy.10 = bf16[128,256]{1,0:T(8,128)(2,1)} copy(bf16[128,256]{1,0:T(8,128)(2,1)} %get-tuple-element.16) | data formatting | bytes 131072
